TPU v7x, 32 devices: a whole 2x2x4 slice. The times are simulated.
32 devices in a mesh: groups: 2 (over y), tensor: 4 (over z), dp: 2 (over x), sub: 2 (over core).
Axes of the slice: x: 2, y: 2, z: 4, core: 2. Of those that a mesh axis runs over, the one named last changes fastest.
Arguments:
- output_gradient: bfloat16 [1024, 8192], P(('groups', 'tensor'), ('dp', 'sub')), parts along dimension 0, may hold values from -6 to 6
- hidden_input: bfloat16 [1024, 28672], P(('groups', 'dp', 'sub'), 'tensor'), parts along dimension 0, may hold values from -6 to 6
- frozen_down_matrix: bfloat16 [28672, 8192], P('tensor', ('dp', 'sub')), may hold values from -0.0625 to 0.0625
- down_factors: bfloat16 [16, 16, 28672], P('groups', None, 'tensor'), parts along dimension 0, may hold values from -0.03125 to 0.03125
- up_factors: bfloat16 [16, 16, 8192], P('groups', None, ('dp', 'sub')), parts along dimension 0, may hold values from -0.13183594 to 0.13183594
- token_adapter_index: int32 [1024], P(('groups', 'dp', 'sub')), parts along dimension 0, may hold values from 0 to 7, never falling along the last dimension, each value on 1 to 256 neighbouring positions
Outputs:
- hidden_input_gradient: bfloat16 [1024, 28672], P(('groups', 'dp', 'sub'), 'tensor'), parts along dimension 0
- down_factor_gradient: float32 [16, 16, 28672], P('groups', None, 'tensor'), parts along dimension 0
- up_factor_gradient: float32 [16, 16, 8192], P('groups', None, ('dp', 'sub')), parts along dimension 0
There are 2 independent parts, one for each index of `groups`. A program takes and returns all parts, laid end to end along the dimension named above; an argument that names none is the same for every part. Nothing has to cross between parts.
Inputs may be any that keep to these rules, and one draw needn't show every extreme that they name: `token_adapter_index`: never falls along the tokens; each adapter has 1 to 256 tokens and some adapter has exactly 256.
All inputs are finite; a program needn't handle non-finite values.
Results may differ from a plain program's by a relative error of at most 0.014.
Values may be sent and summed in bfloat16 or wider, within the bound.
A program may use at most 128 MiB of HBM per device.

v0:
```python
import jax
import jax.numpy as jnp
from jax import lax
from jax.sharding import PartitionSpec as P

ADAPTER_SCALE = 4.0


def contract(left, right, left_dim, right_dim):
    return lax.dot_general(
        left, right, (((left_dim,), (right_dim,)), ((), ())), preferred_element_type=jnp.float32
    )


def on_device(
    output_gradient, hidden_input, frozen_down_matrix, down_factors, up_factors, token_adapter_index
):
    adapter_total = down_factors.shape[0]
    rank_span = down_factors.shape[1]
    down_factor_flat = down_factors.reshape(adapter_total * rank_span, down_factors.shape[2])
    up_factor_flat = up_factors.reshape(adapter_total * rank_span, up_factors.shape[2])
    local_rows = hidden_input.shape[0]
    panels_all = lax.all_gather(output_gradient, "tensor", axis=0, tiled=True)
    frozen_term = lax.psum_scatter(
        contract(panels_all, frozen_down_matrix, 1, 1).astype(jnp.bfloat16),
        ("dp", "sub"),
        scatter_dimension=0,
        tiled=True,
    ).astype(jnp.float32)
    labels = jnp.arange(adapter_total, dtype=jnp.int32)
    member = (token_adapter_index[:, None] == labels[None, :]).astype(jnp.float32)
    mask_cols = jnp.repeat(member, rank_span, axis=1)
    low_part = contract(panels_all, up_factor_flat, 1, 1)
    low_rows = lax.psum_scatter(
        low_part.astype(jnp.bfloat16), ("dp", "sub"), scatter_dimension=0, tiled=True
    ).astype(jnp.float32)
    rank_activation = (mask_cols * low_rows).astype(jnp.bfloat16)
    hidden_input_gradient = (
        frozen_term
        + ADAPTER_SCALE
        * jnp.dot(rank_activation, down_factor_flat, preferred_element_type=jnp.float32)
    ).astype(jnp.bfloat16)
    scale_factor = ADAPTER_SCALE / local_rows
    a_part = scale_factor * contract(rank_activation, hidden_input, 0, 0)
    down_factor_gradient = (
        lax.psum(a_part.astype(jnp.bfloat16), ("dp", "sub"))
        .astype(jnp.float32)
        .reshape(adapter_total, rank_span, -1)
    )
    down_part = contract(hidden_input, down_factor_flat, 1, 1)
    down_full = lax.psum(down_part.astype(jnp.bfloat16), "tensor").astype(jnp.float32)
    down_rank_product = (mask_cols * down_full).astype(jnp.bfloat16)
    down_every = lax.all_gather(down_rank_product, ("dp", "sub"), axis=0, tiled=True)
    slab_rows = output_gradient.shape[0]
    first_slab = lax.axis_index("tensor") * slab_rows
    down_mine = lax.dynamic_slice_in_dim(down_every, first_slab, slab_rows, 0)
    b_total = lax.psum(
        (scale_factor * contract(down_mine, output_gradient, 0, 0)).astype(jnp.bfloat16), "tensor"
    ).astype(jnp.float32)
    up_factor_gradient = b_total.reshape(adapter_total, rank_span, -1)
    return (hidden_input_gradient, down_factor_gradient, up_factor_gradient)


def solution(mesh):
    return jax.shard_map(
        on_device,
        mesh=mesh,
        in_specs=(
            P(("groups", "tensor"), ("dp", "sub")),
            P(("groups", "dp", "sub"), "tensor"),
            P("tensor", ("dp", "sub")),
            P("groups", None, "tensor"),
            P("groups", None, ("dp", "sub")),
            P(("groups", "dp", "sub")),
        ),
        out_specs=(
            P(("groups", "dp", "sub"), "tensor"),
            P("groups", None, "tensor"),
            P("groups", None, ("dp", "sub")),
        ),
        check_vma=False,
    )
```

profile of v0, /device:TPU:3, one launch (start us, length us, event | category | flops | bytes accessed | tf_op | source)
XLA Modules:
  0.0 247.4 jit_solution(16847035948738926389)
XLA Ops:
  7.2 0.0 copy-start
  7.2 0.0 copy-start.4
  7.2 0.0 copy-start.2
  7.2 0.0 all-gather.2.cloned.1.call-start
  7.2 0.7 all-gather.2.cloned.1.call-update
  7.9 0.0 reduce-scatter.5.cloned.1.call-start
  8.0 0.7 copy-done
  8.7 2.1 convolution_convert_fusion.2
  10.8 0.0 copy-start.1
  10.8 16.1 %psum.22 = bf16[128,128]{0,1:T(8,128)(2,1)S(1)} all-reduce(bf16[128,128]{0,1:T(8,128)(2,1)S(1)} %convolution_convert_fusion.2), channel_id=1, replica_groups=mesh['groups'=2,'tensor'=4,'dp'=2,'sub'=2] {'tensor'}, use_global_device_ids=true, to_apply=%region_3.0 | all-reduce | flops 16384 | bytes 65536 | tf_op jit(solution)/shard_map/psum | solution.py:51
  27.0 0.0 copy-done.4
  27.0 30.4 %all-gather.2.cloned.1.call-done = bf16[512,2048]{1,0:T(8,128)(2,1)} async-done(((bf16[128,2048]{1,0:T(8,128)(2,1)}), bf16[512,2048]{1,0:T(8,128)(2,1)}) %all-gather.2.cloned.1.call-update) | async-done | bytes 2097168 | tf_op jit(solution)/shard_map/all_gather | solution.py:23
  57.4 0.0 copy-done.2
  57.4 3.0 %convolution_convert_fusion.1 = bf16[512,128]{1,0:T(8,128)(2,1)} fusion(bf16[512,2048]{1,0:T(8,128)(2,1)} %all-gather.2.cloned.1.call-done, bf16[128,2048]{1,0:T(8,128)(2,1)S(1)} %bitcast.19), kind=kOutput, calls=%fused_computation.8 | convolution fusion | flops 268500992 | bytes 2752512 | tf_op jit(solution)/shard_map/dot_general | solution.py:10
  60.3 0.0 reduce-scatter.5.cloned.1.call-update
  60.4 0.0 all-reduce.5.cloned.1.call-start
  60.4 6.0 %all_gather.7 = bf16[512,128]{0,1:T(8,128)(2,1)S(1)} all-gather(bf16[128,128]{0,1:T(8,128)(2,1)S(1)} %multiply_convert_fusion), channel_id=1, replica_groups=mesh['groups'=2,'tensor'=4,'dp'=2,'sub'=2] {'dp','sub'}, dimensions={0}, use_global_device_ids=true | all-gather | bytes 163840 | tf_op jit(solution)/shard_map/all_gather | solution.py:53
  66.4 0.0 copy-done.1
  66.4 1.1 fusion.3
  67.5 0.0 all-reduce.5.cloned.1.call-update
  67.5 0.0 all-reduce.3.cloned.1.call-start
  67.6 0.1 copy.9
  67.7 9.9 %reduce-scatter.5.cloned.1.call-done = bf16[128,128]{1,0:T(8,128)(2,1)} async-done(((bf16[512,128]{1,0:T(8,128)(2,1)}), bf16[128,128]{1,0:T(8,128)(2,1)}) %reduce-scatter.5.cloned.1.call-update) | async-done | bytes 32784 | tf_op jit(solution)/shard_map/reduce_scatter | solution.py:34
  77.6 3.4 %fusion.2 = bf16[128,7168]{1,0:T(8,128)(2,1)} fusion(bf16[128,7168]{1,0:T(8,128)(2,1)} %param.7, f32[128,128]{1,0:T(8,128)S(1)} %copy.9, bf16[128,128]{1,0:T(8,128)(2,1)} %reduce-scatter.5.cloned.1.call-done), kind=kOutput, calls=%fused_computation.5 | convolution fusion | flops 236765184 | bytes 3768320 | tf_op jit(solution)/shard_map/dot_general | solution.py:10
  81.0 0.0 all-reduce.3.cloned.1.call-update
  81.0 0.0 reduce-scatter.3.cloned.1.call-start
  81.1 22.8 %convolution_convert_fusion = bf16[512,7168]{1,0:T(8,128)(2,1)} fusion(bf16[512,2048]{1,0:T(8,128)(2,1)} %all-gather.2.cloned.1.call-done, bf16[7168,2048]{1,0:T(8,128)(2,1)} %param.8), kind=kOutput, calls=%fused_computation | convolution fusion | flops 15036055552 | bytes 38797312 | tf_op jit(solution)/shard_map/dot_general | solution.py:10
  103.9 0.0 reduce-scatter.3.cloned.1.call-update
  103.9 15.8 %all-reduce.5.cloned.1.call-done = bf16[8,16,2048]{2,1,0:T(8,128)(2,1)} async-done(((bf16[8,16,2048]{2,1,0:T(8,128)(2,1)}), bf16[8,16,2048]{2,1,0:T(8,128)(2,1)}) %all-reduce.5.cloned.1.call-update) | async-done | bytes 524304 | tf_op jit(solution)/shard_map/psum | solution.py:57
  119.7 2.1 reshape.34
  121.8 0.0 copy-start.3
  121.8 47.8 %all-reduce.3.cloned.1.call-done = bf16[8,16,7168]{2,1,0:T(8,128)(2,1)} async-done(((bf16[8,16,7168]{2,1,0:T(8,128)(2,1)}), bf16[8,16,7168]{2,1,0:T(8,128)(2,1)}) %all-reduce.3.cloned.1.call-update) | async-done | bytes 1835024 | tf_op jit(solution)/shard_map/psum | solution.py:46
  169.5 3.7 %reshape.32 = f32[8,16,7168]{2,1,0:T(8,128)} convert(bf16[8,16,7168]{2,1,0:T(8,128)(2,1)} %all-reduce.3.cloned.1.call-done) | non-fusion elementwise | flops 917504 | bytes 5505024 | tf_op jit(solution)/shard_map/reshape | solution.py:48
  173.2 64.3 %reduce-scatter.3.cloned.1.call-done = bf16[128,7168]{1,0:T(8,128)(2,1)} async-done(((bf16[512,7168]{1,0:T(8,128)(2,1)}), bf16[128,7168]{1,0:T(8,128)(2,1)}) %reduce-scatter.3.cloned.1.call-update) | async-done | bytes 1835024 | tf_op jit(solution)/shard_map/reduce_scatter | solution.py:24
  237.6 0.0 copy-done.3
  237.6 3.4 %fusion.1 = bf16[128,7168]{1,0:T(8,128)(2,1)} fusion(bf16[128,7168]{1,0:T(8,128)(2,1)S(1)} %bitcast.15, bf16[128,7168]{1,0:T(8,128)(2,1)} %reduce-scatter.3.cloned.1.call-done, f32[128,128]{1,0:T(8,128)S(1)} %copy.9, bf16[128,128]{1,0:T(8,128)(2,1)S(1)} %copy-done.3), kind=kOutput, calls=%fused_computation.4 | convolution fusion | flops 238600192 | bytes 5603328 | tf_op jit(solution)/shard_map/dot_general | solution.py:41
  (3 shorter events, 0.0 us)
Async XLA Ops:
  7.2 1.5 copy-start
  7.2 19.8 %copy-start.4 = (s32[128]{0:T(128)S(1)}, s32[128]{0:T(128)}, u32[]{:S(2)}) copy-start(s32[128]{0:T(128)} %param.11) | copy-start | bytes 1540
  7.2 50.2 %copy-start.2 = (bf16[8,16,2048]{2,1,0:T(8,128)(2,1)S(1)}, bf16[8,16,2048]{2,1,0:T(8,128)(2,1)}, u32[]{:S(2)}) copy-start(bf16[8,16,2048]{2,1,0:T(8,128)(2,1)} %param.10) | copy-start | bytes 1572868
  7.2 50.2 %all-gather.2.cloned.1.call-start = ((), (), s32[]{:S(2)}) async-start(), calls=%async_computation.2 | async-start | bytes 2621440 | tf_op jit(solution)/shard_map/all_gather | solution.py:23
  7.9 69.7 %reduce-scatter.5.cloned.1.call-start = ((), (), s32[]{:S(2)}) async-start(), calls=%async_computation.4 | async-start | bytes 163840 | tf_op jit(solution)/shard_map/reduce_scatter | solution.py:34
  10.8 55.6 %copy-start.1 = (bf16[128,2048]{1,0:T(8,128)(2,1)S(1)}, bf16[128,2048]{1,0:T(8,128)(2,1)}, u32[]{:S(2)}) copy-start(bf16[128,2048]{1,0:T(8,128)(2,1)} %param.6) | copy-start | bytes 1572868
  60.4 59.3 %all-reduce.5.cloned.1.call-start = ((), (), s32[]{:S(2)}) async-start(), calls=%async_computation.6 | async-start | bytes 1048576 | tf_op jit(solution)/shard_map/psum | solution.py:57
  67.5 102.0 %all-reduce.3.cloned.1.call-start = ((), (), s32[]{:S(2)}) async-start(), calls=%async_computation.5 | async-start | bytes 3670016 | tf_op jit(solution)/shard_map/psum | solution.py:46
  81.0 156.5 %reduce-scatter.3.cloned.1.call-start = ((), (), s32[]{:S(2)}) async-start(), calls=%async_computation.3 | async-start | bytes 9175040 | tf_op jit(solution)/shard_map/reduce_scatter | solution.py:24
  121.8 115.8 %copy-start.3 = (bf16[128,128]{1,0:T(8,128)(2,1)S(1)}, bf16[128,128]{1,0:T(8,128)(2,1)}, u32[]{:S(2)}) copy-start(bf16[128,128]{1,0:T(8,128)(2,1)} %reduce-scatter.5.cloned.1.call-done) | copy-start | bytes 98308
Sparse Core Ops, SparseCore 0:
  9.6 47.7 all-gather.1
  60.5 17.0 reduce-scatter.4
  80.6 38.9 all-reduce.4
  122.6 46.9 all-reduce.2
  172.1 65.4 reduce-scatter.2
where the time goes:
time: 250 us; the launch traced here: 247 us
  waiting for transfers between devices  169 us (68%)
  matrix products  35.7 us (14%)
  blocking collectives  22.1 us (9%)
  between operations  13.9 us (6%)
  other arithmetic  5.84 us (2%)
    reduce_scatter x1, waiting for transfers between devices, on_device(): lax.psum_scatter(contract(panels_all, frozen_down_matrix, 1, 1).astype(jn...  64.3 us
    psum x1, waiting for transfers between devices, on_device(): lax.psum(a_part.astype(jnp.bfloat16), ('dp', 'sub')).astype(jnp.float32)  47.8 us
    dot_general x5, matrix products, contract(): lax.dot_general(left, right, (((left_dim,), (right_dim,)), ((), ())), pre...  32.4 us
    all_gather x1, waiting for transfers between devices, on_device(): panels_all = lax.all_gather(output_gradient, 'tensor', axis=0, tiled=True)  30.4 us
    psum x1, blocking collectives, on_device(): lax.psum(down_part.astype(jnp.bfloat16), 'tensor').astype(jnp.float32)  16.1 us
    psum x1, waiting for transfers between devices, on_device(): lax.psum((scale_factor * contract(down_mine, output_gradient, 0, 0)).asty...  15.8 us
    reduce_scatter x1, waiting for transfers between devices, on_device(): lax.psum_scatter(low_part.astype(jnp.bfloat16), ('dp', 'sub'), scatter_di...  9.9 us
    all_gather x1, blocking collectives, on_device(): lax.all_gather(down_rank_product, ('dp', 'sub'), axis=0, tiled=True)  6 us
  transfers between devices with their start and end apart: 5, of which 5 were waited for; matrix products, arithmetic and copies ran while one was open for 14% of the time, Pallas kernels for 0%

commit v1 on v0

--- a/solution.py
+++ b/solution.py
@@ -1,9 +1,15 @@
+import functools
+
 import jax
 import jax.numpy as jnp
 from jax import lax
+from jax.experimental import pallas as pl
+from jax.experimental.pallas import tpu as pltpu
 from jax.sharding import PartitionSpec as P
 
 ADAPTER_SCALE = 4.0
+CHUNK = 512
+MESH = pl.DeviceIdType.MESH
 
 
 def contract(left, right, left_dim, right_dim):
@@ -12,7 +18,7 @@
     )
 
 
-def on_device(
+def on_device_general(
     output_gradient, hidden_input, frozen_down_matrix, down_factors, up_factors, token_adapter_index
 ):
     adapter_total = down_factors.shape[0]
@@ -61,9 +67,425 @@
     return (hidden_input_gradient, down_factor_gradient, up_factor_gradient)
 
 
+def kernel(
+    scale, og, h, w, a, b, mask, dh_out, da_out, db_out,
+    panels, bv, hv, av, wv, acc, own_l, sib_l, out_c, sib_c, out_x, in_x, in_a, sum_a, dbv,
+    low_p, low_in, low, dn_p, dn_t,
+    load, wload, g_send, g_recv, lp_send, lp_recv, lo_send, lo_recv, dn_send, dn_recv,
+    dt_send, dt_recv, l_send, l_recv, c_send, c_recv, x_send, x_recv, a_recv,
+    d_copy, d_send, d_recv, h_copy, b_copy,
+):
+    g, z = lax.axis_index("groups"), lax.axis_index("tensor")
+    x, c = lax.axis_index("dp"), lax.axis_index("sub")
+    d = 2 * x + c
+    n_chunks = wv.shape[0]
+    half = n_chunks // 2
+    sibling = (g, z, x, 1 - c)
+    across = (g, z, 1 - x, c)
+    plane = (sibling, across, (g, z, 1 - x, 1 - c))
+    line = tuple((g, (z + k) % 4, x, c) for k in (1, 2, 3))
+
+    def send(src, dst, send_sem, recv_sem, device):
+        return pltpu.make_async_remote_copy(
+            src_ref=src, dst_ref=dst, send_sem=send_sem, recv_sem=recv_sem,
+            device_id=device, device_id_type=MESH,
+        )
+
+    def arrived(dst, recv_sem):
+        send(dst, dst, l_send.at[0], recv_sem, sibling).wait_recv()
+
+    def sent(src, send_sem):
+        send(src, src, send_sem, l_recv.at[0], sibling).wait_send()
+
+    loads = [
+        pltpu.make_async_copy(src, dst, load.at[k])
+        for k, (src, dst) in enumerate(((og, panels.at[z]), (b, bv), (h, hv), (a, av)))
+    ]
+    for copy in loads:
+        copy.start()
+
+    def w_copy(j):
+        return pltpu.make_async_copy(w.at[pl.ds(j * CHUNK, CHUNK)], wv.at[j], wload.at[j])
+
+    def column_chunk(t):
+        side = (t // half + 1 + c) % 2
+        return side * half + t % half
+
+    @pl.loop(0, n_chunks)
+    def _(t):
+        w_copy(column_chunk(t)).start()
+
+    barrier = pltpu.get_barrier_semaphore()
+    for peer in plane + line:
+        pl.semaphore_signal(barrier, inc=1, device_id=peer, device_id_type=MESH)
+    pl.semaphore_wait(barrier, 6)
+
+    def own_left():
+        return send(og, panels.at[z], g_send.at[0], g_recv.at[z], (g, z - 1, x, c))
+
+    def own_right():
+        return send(og, panels.at[z], g_send.at[1], g_recv.at[z], (g, z + 1, x, c))
+
+    @pl.when(z > 0)
+    def _():
+        own_left().start()
+
+    @pl.when(z < 3)
+    def _():
+        own_right().start()
+
+    loads[0].wait()
+    loads[1].wait()
+    low_p[...] = contract(panels[z], bv[...], 1, 1).astype(jnp.bfloat16)
+
+    @pl.when(d != z)
+    def _():
+        send(low_p, low_in.at[d], lp_send, lp_recv.at[d], (g, z, z // 2, z % 2)).start()
+
+    loads[2].wait()
+    loads[3].wait()
+
+    def down_step(j, total):
+        cols = pl.ds(pl.multiple_of(j * CHUNK, CHUNK), CHUNK)
+        return total + contract(hv[:, cols], av[:, cols], 1, 1)
+
+    rank_rows = (mask.shape[0], mask.shape[1])
+    dn_p[z] = lax.fori_loop(0, n_chunks, down_step, jnp.zeros(rank_rows, jnp.float32)).astype(
+        jnp.bfloat16
+    )
+    for k, peer in enumerate(line):
+        send(dn_p.at[z], dn_p.at[z], dn_send.at[k], dn_recv.at[z], peer).start()
+
+    @pl.when(d == z)
+    def _():
+        total = low_p[...].astype(jnp.float32)
+        for k in (1, 2, 3):
+            other = (d + k) % 4
+            arrived(low_in.at[other], lp_recv.at[other])
+            total = total + low_in[other].astype(jnp.float32)
+        low[...] = (mask[...] * total).astype(jnp.bfloat16)
+        for k, peer in enumerate(line):
+            send(low, low, lo_send.at[k], lo_recv, peer).start()
+
+    @pl.when(d != z)
+    def _():
+        arrived(low, lo_recv)
+
+    def give_sibling(k, t, value):
+        out_c[k, t] = value.astype(jnp.bfloat16)
+        send(out_c.at[k, t], sib_c.at[k, t], c_send.at[k, t], c_recv.at[k, t], sibling).start()
+
+    def add_sibling(k, t, value):
+        arrived(sib_c.at[k, t], c_recv.at[k, t])
+        out_x[k, t] = (value + sib_c[k, t].astype(jnp.float32)).astype(jnp.bfloat16)
+
+    low_t = low[...].astype(jnp.float32).T.astype(jnp.bfloat16)
+
+    def a_part(t):
+        cols = pl.ds(pl.multiple_of(column_chunk(t) * CHUNK, CHUNK), CHUNK)
+        return scale * jnp.dot(low_t, hv[:, cols], preferred_element_type=jnp.float32)
+
+    @pl.loop(0, half)
+    def _(t):
+        give_sibling(2, t, a_part(t))
+
+    @pl.loop(0, half)
+    def _(t):
+        add_sibling(2, t, a_part(t + half))
+        send(out_x.at[2, t], in_a.at[t], x_send.at[2, t], a_recv.at[t], across).start()
+
+    def forward(block):
+        @pl.when((block < z) & (z < 3))
+        def _():
+            send(
+                panels.at[block], panels.at[block], g_send.at[2 + block], g_recv.at[block],
+                (g, z + 1, x, c),
+            ).start()
+
+        @pl.when((block > z) & (z > 0))
+        def _():
+            send(
+                panels.at[block], panels.at[block], g_send.at[2 + block], g_recv.at[block],
+                (g, z - 1, x, c),
+            ).start()
+
+    def step(block, first):
+        k = block % 2
+        here = block // 2 == x
+
+        def product(j):
+            return contract(panels[block], wv[j], 1, 1)
+
+        @pl.loop(0, half)
+        def _(t):
+            j = column_chunk(t)
+            if first:
+                w_copy(j).wait()
+            value = product(j)
+
+            @pl.when(here & (k == c))
+            def _():
+                acc[j] = value.astype(jnp.bfloat16)
+
+            @pl.when(here & (k != c))
+            def _():
+                own_l[j] = value.astype(jnp.bfloat16)
+                send(own_l.at[j], sib_l.at[j], l_send.at[j], l_recv.at[j], sibling).start()
+
+            @pl.when(block // 2 != x)
+            def _():
+                give_sibling(k, t, value)
+
+        @pl.loop(0, half)
+        def _(t):
+            j = column_chunk(t + half)
+            if first:
+                w_copy(j).wait()
+            value = product(j)
+
+            @pl.when(here & (k == c))
+            def _():
+                acc[j] = value.astype(jnp.bfloat16)
+
+            @pl.when(here & (k != c))
+            def _():
+                own_l[j] = value.astype(jnp.bfloat16)
+                send(own_l.at[j], sib_l.at[j], l_send.at[j], l_recv.at[j], sibling).start()
+
+            @pl.when(block // 2 != x)
+            def _():
+                add_sibling(k, t, value)
+                send(
+                    out_x.at[k, t], in_x.at[j], x_send.at[k, t], x_recv.at[j], (g, z, 1 - x, k)
+                ).start()
+
+    end = 1 - (z % 3 + 1) // 2
+    mids = (z, z + 1 - 2 * x, z - 1 + 2 * x, 3 * (2 - z))
+    order = [end * (i + (z // 3) * (3 - 2 * i)) + (1 - end) * mids[i] for i in range(4)]
+
+    step(order[0], True)
+    arrived(panels.at[order[1]], g_recv.at[order[1]])
+    forward(order[1])
+
+    @pl.when(end == 0)
+    def _():
+        arrived(panels.at[order[2]], g_recv.at[order[2]])
+        forward(order[2])
+
+    step(order[1], False)
+
+    for k in (1, 2, 3):
+        other = (z + k) % 4
+        arrived(dn_p.at[other], dn_recv.at[other])
+    down = jnp.zeros(rank_rows, jnp.float32)
+    for k in range(4):
+        down = down + dn_p[k].astype(jnp.float32)
+    dn_t[d] = (mask[...] * down).T.astype(jnp.bfloat16)
+    for k, peer in enumerate(plane):
+        send(dn_t.at[d], dn_t.at[d], dt_send.at[k], dt_recv.at[d], peer).start()
+
+    @pl.when(end == 1)
+    def _():
+        arrived(panels.at[order[2]], g_recv.at[order[2]])
+
+    step(order[2], False)
+    arrived(panels.at[order[3]], g_recv.at[order[3]])
+    forward(order[3])
+    step(order[3], False)
+
+    for k in (1, 2, 3):
+        other = (d + k) % 4
+        arrived(dn_t.at[other], dt_recv.at[other])
+
+    @pl.loop(0, dbv.shape[1] // CHUNK)
+    def _(j):
+        cols = pl.ds(pl.multiple_of(j * CHUNK, CHUNK), CHUNK)
+        total = jnp.dot(dn_t[0], panels[0, :, cols], preferred_element_type=jnp.float32)
+        for k in (1, 2, 3):
+            total += jnp.dot(dn_t[k], panels[k, :, cols], preferred_element_type=jnp.float32)
+        dbv[:, cols] = scale * total
+
+    db_copy = pltpu.make_async_copy(dbv, db_out, b_copy)
+    db_copy.start()
+
+    def a_cols(t):
+        return pl.ds(pl.multiple_of((c * half + t) * CHUNK, CHUNK), CHUNK)
+
+    def a_copy(t):
+        return pltpu.make_async_copy(sum_a.at[t], da_out.at[:, a_cols(t)], d_copy.at[t])
+
+    def a_give(t):
+        where = da_out.at[:, a_cols(t)]
+        return send(sum_a.at[t], where, d_send.at[t], d_recv.at[t], sibling)
+
+    @pl.loop(0, half)
+    def _(t):
+        arrived(in_a.at[t], a_recv.at[t])
+        sum_a[t] = (out_x[2, t].astype(jnp.float32) + in_a[t].astype(jnp.float32)).astype(
+            jnp.bfloat16
+        )
+        a_copy(t).start()
+        a_give(t).start()
+
+    def h_out(j):
+        cols = pl.ds(pl.multiple_of(j * CHUNK, CHUNK), CHUNK)
+        return pltpu.make_async_copy(acc.at[j], dh_out.at[:, cols], h_copy.at[j])
+
+    @pl.loop(0, n_chunks)
+    def _(t):
+        j = (t % 2) * half + t // 2
+        cols = pl.ds(pl.multiple_of(j * CHUNK, CHUNK), CHUNK)
+        rank_term = jnp.dot(low[...], av[:, cols], preferred_element_type=jnp.float32)
+        arrived(sib_l.at[j], l_recv.at[j])
+        arrived(in_x.at[j], x_recv.at[j])
+        total = acc[j].astype(jnp.float32) + sib_l[j].astype(jnp.float32)
+        total = total + in_x[j].astype(jnp.float32) + ADAPTER_SCALE * rank_term
+        acc[j] = total.astype(jnp.bfloat16)
+        h_out(j).start()
+
+    @pl.loop(0, n_chunks)
+    def _(j):
+        h_out(j).wait()
+        sent(own_l.at[j], l_send.at[j])
+
+    @pl.loop(0, half)
+    def _(t):
+        a_copy(t).wait()
+        a_give(t).wait_send()
+        other = pl.ds(pl.multiple_of(((1 - c) * half + t) * CHUNK, CHUNK), CHUNK)
+        arrived(da_out.at[:, other], d_recv.at[t])
+        for k in range(3):
+            sent(out_c.at[k, t], c_send.at[k, t])
+            sent(out_x.at[k, t], x_send.at[k, t])
+
+    db_copy.wait()
+    for k in range(3):
+        sent(dn_p.at[z], dn_send.at[k])
+        sent(dn_t.at[d], dt_send.at[k])
+
+    @pl.when(d == z)
+    def _():
+        for k in range(3):
+            sent(low, lo_send.at[k])
+
+    @pl.when(d != z)
+    def _():
+        sent(low_p, lp_send)
+
+    @pl.when(z > 0)
+    def _():
+        own_left().wait_send()
+
+    @pl.when(z < 3)
+    def _():
+        own_right().wait_send()
+
+    @pl.when(end == 0)
+    def _():
+        for k in (1, 2, 3):
+            sent(panels.at[order[k]], g_send.at[2 + order[k]])
+
+
+def on_device_small(
+    output_gradient, hidden_input, frozen_down_matrix, down_factors, up_factors, token_adapter_index
+):
+    adapters, rank, hidden = down_factors.shape
+    ranks = adapters * rank
+    rows, features = output_gradient.shape
+    n_chunks = hidden // CHUNK
+    half = n_chunks // 2
+    labels = jnp.arange(adapters, dtype=jnp.int32)
+    member = (token_adapter_index[:, None] == labels[None, :]).astype(jnp.float32)
+    mask_cols = jnp.repeat(member, rank, axis=1)
+    bf16, f32 = jnp.bfloat16, jnp.float32
+    dma = pltpu.SemaphoreType.DMA
+
+    def vmem(*shape, dtype=bf16):
+        return pltpu.VMEM(shape, dtype)
+
+    flops = 2 * 4 * rows * features * hidden
+    hidden_gradient, down_gradient, up_gradient = pl.pallas_call(
+        functools.partial(kernel, ADAPTER_SCALE / rows),
+        out_shape=(
+            jax.ShapeDtypeStruct((rows, hidden), bf16),
+            jax.ShapeDtypeStruct((ranks, hidden), bf16),
+            jax.ShapeDtypeStruct((ranks, features), f32),
+        ),
+        in_specs=[pl.BlockSpec(memory_space=pl.ANY)] * 5
+        + [pl.BlockSpec(memory_space=pltpu.VMEM)],
+        out_specs=[pl.BlockSpec(memory_space=pl.ANY)] * 3,
+        scratch_shapes=[
+            vmem(4, rows, features),
+            vmem(ranks, features),
+            vmem(rows, hidden),
+            vmem(ranks, hidden),
+            vmem(n_chunks, CHUNK, features),
+            vmem(n_chunks, rows, CHUNK),
+            vmem(n_chunks, rows, CHUNK),
+            vmem(n_chunks, rows, CHUNK),
+            vmem(3, half, rows, CHUNK),
+            vmem(3, half, rows, CHUNK),
+            vmem(3, half, rows, CHUNK),
+            vmem(n_chunks, rows, CHUNK),
+            vmem(half, rows, CHUNK),
+            vmem(half, rows, CHUNK),
+            vmem(ranks, features, dtype=f32),
+            vmem(rows, ranks),
+            vmem(4, rows, ranks),
+            vmem(rows, ranks),
+            vmem(4, rows, ranks),
+            vmem(4, ranks, rows),
+            dma((4,)),
+            dma((n_chunks,)),
+            dma((6,)),
+            dma((4,)),
+            dma,
+            dma((4,)),
+            dma((3,)),
+            dma,
+            dma((3,)),
+            dma((4,)),
+            dma((3,)),
+            dma((4,)),
+            dma((n_chunks,)),
+            dma((n_chunks,)),
+            dma((3, half)),
+            dma((3, half)),
+            dma((3, half)),
+            dma((n_chunks,)),
+            dma((half,)),
+            dma((half,)),
+            dma((half,)),
+            dma((half,)),
+            dma((n_chunks,)),
+            dma,
+        ],
+        compiler_params=pltpu.CompilerParams(
+            collective_id=0, has_side_effects=True, vmem_limit_bytes=60 << 20
+        ),
+        cost_estimate=pl.CostEstimate(
+            flops=flops, bytes_accessed=2 * features * hidden, transcendentals=0
+        ),
+    )(
+        output_gradient,
+        hidden_input,
+        frozen_down_matrix,
+        down_factors.reshape(ranks, hidden),
+        up_factors.reshape(ranks, features),
+        mask_cols,
+    )
+    return (
+        hidden_gradient,
+        down_gradient.astype(f32).reshape(adapters, rank, hidden),
+        up_gradient.reshape(adapters, rank, features),
+    )
+
+
 def solution(mesh):
+    sizes = tuple(mesh.shape[n] for n in ("tensor", "dp", "sub"))
+    fits = sizes == (4, 2, 2)
     return jax.shard_map(
-        on_device,
+        on_device_small if fits else on_device_general,
         mesh=mesh,
         in_specs=(
             P(("groups", "tensor"), ("dp", "sub")),

time: 250 us -> 112 us (0.45)
  waiting for transfers between devices: 169 us -> 0 us
  Pallas kernels: 0 us -> 103 us
  matrix products: 35.7 us -> 0 us
  blocking collectives: 22.1 us -> 0 us
  between operations: 13.9 us -> 0.65 us
  local copies, waits for them, and re-layouts: 0.81 us -> 3.6 us
    pallas_call x0 -> x1, Pallas kernels: none -> 103 us  [on_device_small(): pl.pallas_call(functools.partial(kernel, ADAPTER_SCALE / rows), out_shape...]
    reduce_scatter x2 -> x0, waiting for transfers between devices: 74.2 us -> none  [the longest x1 64.3 us: on_device(): lax.psum_scatter(contract(panels_all, frozen_down_matrix, 1, 1).astype(jn...]
    psum x2 -> x0, waiting for transfers between devices: 63.5 us -> none  [the longest x1 47.8 us: on_device(): lax.psum(a_part.astype(jnp.bfloat16), ('dp', 'sub')).astype(jnp.float32)]
    dot_general x6 -> x0, matrix products: 35.7 us -> none  [the longest x5 32.4 us: contract(): lax.dot_general(left, right, (((left_dim,), (right_dim,)), ((), ())), pre...]
    all_gather x1 -> x0, waiting for transfers between devices: 30.4 us -> none  [on_device(): panels_all = lax.all_gather(output_gradient, 'tensor', axis=0, tiled=True)]
    psum x1 -> x0, blocking collectives: 16.1 us -> none  [on_device(): lax.psum(down_part.astype(jnp.bfloat16), 'tensor').astype(jnp.float32)]
    all_gather x1 -> x0, blocking collectives: 6 us -> none  [on_device(): lax.all_gather(down_rank_product, ('dp', 'sub'), axis=0, tiled=True)]
    reshape x2 -> x1, other arithmetic: 5.82 us -> 3.84 us  [on_device_small(): down_gradient.astype(f32).reshape(adapters, rank, hidden)]
  transfers between devices with their start and end apart: 5 -> 0, of which waited for: 5 -> 0; matrix products, arithmetic and copies ran while one was open for 14% -> 0% of each run, Pallas kernels for 0% -> 0%
where the time goes in v1:
time: 112 us; the launch traced here: 111 us
  Pallas kernels  103 us (92%)
  other arithmetic  4.5 us (4%)
  local copies, waits for them, and re-layouts  3.6 us (3%)
    pallas_call x1, Pallas kernels, on_device_small(): pl.pallas_call(functools.partial(kernel, ADAPTER_SCALE / rows), out_shape...  103 us
    reshape x1, other arithmetic, on_device_small(): down_gradient.astype(f32).reshape(adapters, rank, hidden)  3.84 us
    unnamed x6, local copies, waits for them, and re-layouts  2.86 us

profile of v1, /device:TPU:3, one launch (start us, length us, event | category | flops | bytes accessed | tf_op | source)
XLA Modules:
  0.0 111.3 jit_solution(13327713198662535957)
XLA Ops:
  0.6 0.7 fusion
  1.3 0.7 copy.9.mask
  2.0 102.6 %shard_map.85 = (bf16[128,7168]{1,0:T(8,128)(2,1)}, bf16[128,7168]{1,0:T(8,128)(2,1)}, f32[128,2048]{1,0:T(8,128)}) custom-call(bf16[128,2048]{1,0:T(8,128)(2,1)} %og.1, bf16[128,7168]{1,0:T(8,128)(2,1)} %h.1, bf16[7168,2048]{1,0:T(8,128)(2,1)} %w.1, bf16[128,7168]{1,0:T(8,128)(2,1)} %bitcast.9, bf16[128,2048]{1,0:T(8,128)(2,1)} %bitcast.10, ...), custom_call_target="tpu_custom_call" | custom-call | flops 15032385536 | bytes 29360128 | tf_op jit(solution)/shard_map/pallas_call | solution.py:407
  104.6 0.0 copy-start
  104.6 3.8 %convert.1 = f32[8,16,7168]{2,1,0:T(8,128)} convert(bf16[8,16,7168]{2,1,0:T(8,128)(2,1)} %bitcast.6) | non-fusion elementwise | flops 917504 | bytes 5505024 | tf_op jit(solution)/shard_map/reshape | solution.py:479
  108.5 0.0 copy-done
  108.5 0.0 copy-start.1
  108.5 1.2 %copy.12 = bf16[128,7168]{1,0:T(8,128)(2,1)} copy(bf16[128,7168]{1,0:T(8,128)(2,1)S(1)} %copy-done) | data formatting | bytes 3670016
  109.7 0.7 copy-done.1
  110.4 1.0 copy.13
  (1 shorter events, 0.0 us)
Async XLA Ops:
  104.6 3.9 %copy-start = (bf16[128,7168]{1,0:T(8,128)(2,1)S(1)}, bf16[128,7168]{1,0:T(8,128)(2,1)}, u32[]{:S(2)}) copy-start(bf16[128,7168]{1,0:T(8,128)(2,1)} %get-tuple-element.12) | copy-start | bytes 5505028
  108.5 1.9 %copy-start.1 = (f32[128,2048]{1,0:T(8,128)S(1)}, f32[128,2048]{1,0:T(8,128)}, u32[]{:S(2)}) copy-start(f32[128,2048]{1,0:T(8,128)} %get-tuple-element.8) | copy-start | bytes 3145732

commit v2 on v1

--- a/solution.py
+++ b/solution.py
@@ -68,9 +68,9 @@
 
 
 def kernel(
-    scale, og, h, w, a, b, mask, dh_out, da_out, db_out,
-    panels, bv, hv, av, wv, acc, own_l, sib_l, out_c, sib_c, out_x, in_x, in_a, sum_a, dbv,
-    low_p, low_in, low, dn_p, dn_t,
+    scale, adapters, og, h, w, a, b, labels, dh_out, da_out, db_out,
+    panels, bv, hv, av, wv, acc, own_l, sib_l, out_c, sib_c, out_x, in_x, in_a, sum_a, sib_a, dav, dbv,
+    low_p, low_in, low_t, low, dn_p, dn_t,
     load, wload, g_send, g_recv, lp_send, lp_recv, lo_send, lo_recv, dn_send, dn_recv,
     dt_send, dt_recv, l_send, l_recv, c_send, c_recv, x_send, x_recv, a_recv,
     d_copy, d_send, d_recv, h_copy, b_copy,
@@ -111,10 +111,6 @@
         side = (t // half + 1 + c) % 2
         return side * half + t % half
 
-    @pl.loop(0, n_chunks)
-    def _(t):
-        w_copy(column_chunk(t)).start()
-
     barrier = pltpu.get_barrier_semaphore()
     for peer in plane + line:
         pl.semaphore_signal(barrier, inc=1, device_id=peer, device_id_type=MESH)
@@ -134,9 +130,12 @@
     def _():
         own_right().start()
 
+    rank_rows = (low_t.shape[0], low_t.shape[1])
+    rank_of_row = lax.broadcasted_iota(jnp.int32, rank_rows, 0) // (rank_rows[0] // adapters)
+    mask = jnp.where(rank_of_row == labels[...], 1.0, 0.0)
     loads[0].wait()
     loads[1].wait()
-    low_p[...] = contract(panels[z], bv[...], 1, 1).astype(jnp.bfloat16)
+    low_p[...] = contract(bv[...], panels[z], 1, 1).astype(jnp.bfloat16)
 
     @pl.when(d != z)
     def _():
@@ -145,54 +144,57 @@
     loads[2].wait()
     loads[3].wait()
 
+    @pl.loop(0, n_chunks)
+    def _(t):
+        w_copy(column_chunk(t)).start()
+
+    @pl.when(d == z)
+    def _():
+        total = low_p[...].astype(jnp.float32)
+        for k in (1, 2, 3):
+            other = (d + k) % 4
+            arrived(low_in.at[other], lp_recv.at[other])
+            total = total + low_in[other].astype(jnp.float32)
+        low_t[...] = (mask * total).astype(jnp.bfloat16)
+        for k, peer in enumerate(line):
+            send(low_t, low_t, lo_send.at[k], lo_recv, peer).start()
+
+    @pl.when(d != z)
+    def _():
+        arrived(low_t, lo_recv)
+
+    def give_sibling(k, t, value):
+        out_c[k, t] = value.astype(jnp.bfloat16)
+        send(out_c.at[k, t], sib_c.at[k, t], c_send.at[k, t], c_recv.at[k, t], sibling).start()
+
+    def add_sibling(k, t, value):
+        arrived(sib_c.at[k, t], c_recv.at[k, t])
+        out_x[k, t] = (value + sib_c[k, t].astype(jnp.float32)).astype(jnp.bfloat16)
+
+    def a_part(t):
+        cols = pl.ds(pl.multiple_of(column_chunk(t) * CHUNK, CHUNK), CHUNK)
+        return scale * jnp.dot(low_t[...], hv[:, cols], preferred_element_type=jnp.float32)
+
+    @pl.loop(0, half)
+    def _(t):
+        give_sibling(2, t, a_part(t))
+
+    @pl.loop(0, half)
+    def _(t):
+        add_sibling(2, t, a_part(t + half))
+        send(out_x.at[2, t], in_a.at[t], x_send.at[2, t], a_recv.at[t], across).start()
+
+    low[...] = low_t[...].astype(jnp.float32).T.astype(jnp.bfloat16)
+
     def down_step(j, total):
         cols = pl.ds(pl.multiple_of(j * CHUNK, CHUNK), CHUNK)
-        return total + contract(hv[:, cols], av[:, cols], 1, 1)
-
-    rank_rows = (mask.shape[0], mask.shape[1])
+        return total + contract(av[:, cols], hv[:, cols], 1, 1)
+
     dn_p[z] = lax.fori_loop(0, n_chunks, down_step, jnp.zeros(rank_rows, jnp.float32)).astype(
         jnp.bfloat16
     )
     for k, peer in enumerate(line):
         send(dn_p.at[z], dn_p.at[z], dn_send.at[k], dn_recv.at[z], peer).start()
-
-    @pl.when(d == z)
-    def _():
-        total = low_p[...].astype(jnp.float32)
-        for k in (1, 2, 3):
-            other = (d + k) % 4
-            arrived(low_in.at[other], lp_recv.at[other])
-            total = total + low_in[other].astype(jnp.float32)
-        low[...] = (mask[...] * total).astype(jnp.bfloat16)
-        for k, peer in enumerate(line):
-            send(low, low, lo_send.at[k], lo_recv, peer).start()
-
-    @pl.when(d != z)
-    def _():
-        arrived(low, lo_recv)
-
-    def give_sibling(k, t, value):
-        out_c[k, t] = value.astype(jnp.bfloat16)
-        send(out_c.at[k, t], sib_c.at[k, t], c_send.at[k, t], c_recv.at[k, t], sibling).start()
-
-    def add_sibling(k, t, value):
-        arrived(sib_c.at[k, t], c_recv.at[k, t])
-        out_x[k, t] = (value + sib_c[k, t].astype(jnp.float32)).astype(jnp.bfloat16)
-
-    low_t = low[...].astype(jnp.float32).T.astype(jnp.bfloat16)
-
-    def a_part(t):
-        cols = pl.ds(pl.multiple_of(column_chunk(t) * CHUNK, CHUNK), CHUNK)
-        return scale * jnp.dot(low_t, hv[:, cols], preferred_element_type=jnp.float32)
-
-    @pl.loop(0, half)
-    def _(t):
-        give_sibling(2, t, a_part(t))
-
-    @pl.loop(0, half)
-    def _(t):
-        add_sibling(2, t, a_part(t + half))
-        send(out_x.at[2, t], in_a.at[t], x_send.at[2, t], a_recv.at[t], across).start()
 
     def forward(block):
         @pl.when((block < z) & (z < 3))
@@ -209,7 +211,7 @@
                 (g, z - 1, x, c),
             ).start()
 
-    def step(block, first):
+    def step(block, first, between=None):
         k = block % 2
         here = block // 2 == x
 
@@ -236,6 +238,9 @@
             def _():
                 give_sibling(k, t, value)
 
+        if between is not None:
+            between()
+
         @pl.loop(0, half)
         def _(t):
             j = column_chunk(t + half)
@@ -263,16 +268,16 @@
     mids = (z, z + 1 - 2 * x, z - 1 + 2 * x, 3 * (2 - z))
     order = [end * (i + (z // 3) * (3 - 2 * i)) + (1 - end) * mids[i] for i in range(4)]
 
+    def take(block):
+        arrived(panels.at[block], g_recv.at[block])
+        forward(block)
+
+    @pl.when(end == 0)
+    def _():
+        take(order[1])
+        take(order[2])
+
     step(order[0], True)
-    arrived(panels.at[order[1]], g_recv.at[order[1]])
-    forward(order[1])
-
-    @pl.when(end == 0)
-    def _():
-        arrived(panels.at[order[2]], g_recv.at[order[2]])
-        forward(order[2])
-
-    step(order[1], False)
 
     for k in (1, 2, 3):
         other = (z + k) % 4
@@ -280,18 +285,54 @@
     down = jnp.zeros(rank_rows, jnp.float32)
     for k in range(4):
         down = down + dn_p[k].astype(jnp.float32)
-    dn_t[d] = (mask[...] * down).T.astype(jnp.bfloat16)
+    dn_t[d] = (mask * down).astype(jnp.bfloat16)
     for k, peer in enumerate(plane):
         send(dn_t.at[d], dn_t.at[d], dt_send.at[k], dt_recv.at[d], peer).start()
 
     @pl.when(end == 1)
     def _():
-        arrived(panels.at[order[2]], g_recv.at[order[2]])
+        take(order[1])
+
+    def take_last():
+        @pl.when(end == 0)
+        def _():
+            take(order[3])
+
+    step(order[1], False, take_last)
+
+    @pl.when(end == 1)
+    def _():
+        take(order[2])
 
     step(order[2], False)
-    arrived(panels.at[order[3]], g_recv.at[order[3]])
-    forward(order[3])
+
+    def a_copy(j):
+        cols = pl.ds(pl.multiple_of(j * CHUNK, CHUNK), CHUNK)
+        return pltpu.make_async_copy(dav.at[j], da_out.at[:, cols], d_copy.at[j])
+
+    def a_give(t):
+        return send(sum_a.at[t], sib_a.at[t], d_send.at[t], d_recv.at[t], sibling)
+
+    @pl.loop(0, half)
+    def _(t):
+        arrived(in_a.at[t], a_recv.at[t])
+        total = out_x[2, t].astype(jnp.float32) + in_a[t].astype(jnp.float32)
+        sum_a[t] = total.astype(jnp.bfloat16)
+        a_give(t).start()
+        dav[c * half + t] = sum_a[t].astype(jnp.float32)
+        a_copy(c * half + t).start()
+
+    @pl.when(end == 1)
+    def _():
+        take(order[3])
+
     step(order[3], False)
+
+    @pl.loop(0, half)
+    def _(t):
+        arrived(sib_a.at[t], d_recv.at[t])
+        dav[(1 - c) * half + t] = sib_a[t].astype(jnp.float32)
+        a_copy((1 - c) * half + t).start()
 
     for k in (1, 2, 3):
         other = (d + k) % 4
@@ -307,25 +348,6 @@
 
     db_copy = pltpu.make_async_copy(dbv, db_out, b_copy)
     db_copy.start()
-
-    def a_cols(t):
-        return pl.ds(pl.multiple_of((c * half + t) * CHUNK, CHUNK), CHUNK)
-
-    def a_copy(t):
-        return pltpu.make_async_copy(sum_a.at[t], da_out.at[:, a_cols(t)], d_copy.at[t])
-
-    def a_give(t):
-        where = da_out.at[:, a_cols(t)]
-        return send(sum_a.at[t], where, d_send.at[t], d_recv.at[t], sibling)
-
-    @pl.loop(0, half)
-    def _(t):
-        arrived(in_a.at[t], a_recv.at[t])
-        sum_a[t] = (out_x[2, t].astype(jnp.float32) + in_a[t].astype(jnp.float32)).astype(
-            jnp.bfloat16
-        )
-        a_copy(t).start()
-        a_give(t).start()
 
     def h_out(j):
         cols = pl.ds(pl.multiple_of(j * CHUNK, CHUNK), CHUNK)
@@ -351,9 +373,8 @@
     @pl.loop(0, half)
     def _(t):
         a_copy(t).wait()
+        a_copy(half + t).wait()
         a_give(t).wait_send()
-        other = pl.ds(pl.multiple_of(((1 - c) * half + t) * CHUNK, CHUNK), CHUNK)
-        arrived(da_out.at[:, other], d_recv.at[t])
         for k in range(3):
             sent(out_c.at[k, t], c_send.at[k, t])
             sent(out_x.at[k, t], x_send.at[k, t])
@@ -366,7 +387,7 @@
     @pl.when(d == z)
     def _():
         for k in range(3):
-            sent(low, lo_send.at[k])
+            sent(low_t, lo_send.at[k])
 
     @pl.when(d != z)
     def _():
@@ -394,9 +415,6 @@
     rows, features = output_gradient.shape
     n_chunks = hidden // CHUNK
     half = n_chunks // 2
-    labels = jnp.arange(adapters, dtype=jnp.int32)
-    member = (token_adapter_index[:, None] == labels[None, :]).astype(jnp.float32)
-    mask_cols = jnp.repeat(member, rank, axis=1)
     bf16, f32 = jnp.bfloat16, jnp.float32
     dma = pltpu.SemaphoreType.DMA
 
@@ -405,10 +423,10 @@
 
     flops = 2 * 4 * rows * features * hidden
     hidden_gradient, down_gradient, up_gradient = pl.pallas_call(
-        functools.partial(kernel, ADAPTER_SCALE / rows),
+        functools.partial(kernel, ADAPTER_SCALE / rows, adapters),
         out_shape=(
             jax.ShapeDtypeStruct((rows, hidden), bf16),
-            jax.ShapeDtypeStruct((ranks, hidden), bf16),
+            jax.ShapeDtypeStruct((ranks, hidden), f32),
             jax.ShapeDtypeStruct((ranks, features), f32),
         ),
         in_specs=[pl.BlockSpec(memory_space=pl.ANY)] * 5
@@ -429,11 +447,14 @@
             vmem(n_chunks, rows, CHUNK),
             vmem(half, rows, CHUNK),
             vmem(half, rows, CHUNK),
+            vmem(half, rows, CHUNK),
+            vmem(n_chunks, rows, CHUNK, dtype=f32),
             vmem(ranks, features, dtype=f32),
+            vmem(ranks, rows),
+            vmem(4, ranks, rows),
+            vmem(ranks, rows),
             vmem(rows, ranks),
-            vmem(4, rows, ranks),
-            vmem(rows, ranks),
-            vmem(4, rows, ranks),
+            vmem(4, ranks, rows),
             vmem(4, ranks, rows),
             dma((4,)),
             dma((n_chunks,)),
@@ -454,7 +475,7 @@
             dma((3, half)),
             dma((n_chunks,)),
             dma((half,)),
-            dma((half,)),
+            dma((n_chunks,)),
             dma((half,)),
             dma((half,)),
             dma((n_chunks,)),
@@ -472,11 +493,11 @@
         frozen_down_matrix,
         down_factors.reshape(ranks, hidden),
         up_factors.reshape(ranks, features),
-        mask_cols,
+        token_adapter_index.reshape(1, rows),
     )
     return (
         hidden_gradient,
-        down_gradient.astype(f32).reshape(adapters, rank, hidden),
+        down_gradient.reshape(adapters, rank, hidden),
         up_gradient.reshape(adapters, rank, features),
     )
 

time: 112 us -> 104 us (0.929)
  Pallas kernels: 103 us -> 96.9 us
  other arithmetic: 4.5 us -> 0 us
  local copies, waits for them, and re-layouts: 3.6 us -> 5.93 us
    pallas_call x1, Pallas kernels: 103 us -> 96.9 us  [on_device_small(): pl.pallas_call(functools.partial(kernel, ADAPTER_SCALE / rows, adapters),...]
    reshape x1 -> x0, other arithmetic: 3.84 us -> none  [on_device_small(): down_gradient.astype(f32).reshape(adapters, rank, hidden)]
    unnamed x6 -> x7, local copies, waits for them, and re-layouts: 2.86 us -> 5.93 us
where the time goes in v2:
time: 104 us; the launch traced here: 103 us
  Pallas kernels  96.9 us (93%)
  local copies, waits for them, and re-layouts  5.93 us (6%)
    pallas_call x1, Pallas kernels, on_device_small(): pl.pallas_call(functools.partial(kernel, ADAPTER_SCALE / rows, adapters),...  96.9 us
    unnamed x7, local copies, waits for them, and re-layouts  5.93 us

profile of v2, /device:TPU:3, one launch (start us, length us, event | category | flops | bytes accessed | tf_op | source)
XLA Modules:
  0.0 103.4 jit_solution(4835447093281214007)
XLA Ops:
  0.6 96.9 %shard_map.85 = (bf16[128,7168]{1,0:T(8,128)(2,1)}, f32[128,7168]{1,0:T(8,128)}, f32[128,2048]{1,0:T(8,128)}) custom-call(bf16[128,2048]{1,0:T(8,128)(2,1)} %og.1, bf16[128,7168]{1,0:T(8,128)(2,1)} %h.1, bf16[7168,2048]{1,0:T(8,128)(2,1)} %w.1, bf16[128,7168]{1,0:T(8,128)(2,1)} %bitcast.7, bf16[128,2048]{1,0:T(8,128)(2,1)} %bitcast.8, s32[1,128]{1,0:T(1,128)} %bitcast.9), custom_call_target="tpu_custom_call" | custom-call | flops 15032385536 | bytes 29360128 | tf_op jit(solution)/shard_map/pallas_call | solution.py:425
  97.5 0.0 copy-start
  97.5 3.0 %copy.12 = bf16[128,7168]{1,0:T(8,128)(2,1)} copy(bf16[128,7168]{1,0:T(8,128)(2,1)} %get-tuple-element.12) | data formatting | bytes 3670016
  100.5 0.0 copy-done
  100.5 0.0 copy-start.1
  100.5 1.8 %copy.13 = f32[8,16,7168]{2,1,0:T(8,128)} copy(f32[8,16,7168]{2,1,0:T(8,128)S(1)} %bitcast.5) | data formatting | bytes 7340032
  102.3 0.1 copy-done.1
  102.5 1.0 copy.14
Async XLA Ops:
  97.5 3.0 %copy-start = (f32[128,7168]{1,0:T(8,128)S(1)}, f32[128,7168]{1,0:T(8,128)}, u32[]{:S(2)}) copy-start(f32[128,7168]{1,0:T(8,128)} %get-tuple-element.7) | copy-start | bytes 11010052
  100.5 2.0 %copy-start.1 = (f32[128,2048]{1,0:T(8,128)S(1)}, f32[128,2048]{1,0:T(8,128)}, u32[]{:S(2)}) copy-start(f32[128,2048]{1,0:T(8,128)} %get-tuple-element.8) | copy-start | bytes 3145732
